TPU v7x, 256 devices: a whole 4x4x8 slice. The times are simulated.
256 devices in a mesh: dp: 8 (over z_lo, y), section: 8 (over z_hi, core), fsdp: 4 (over x).
Axes of the slice: x: 4, y: 4, z: 8 (z_hi: 4, z_lo: 2; z = z_hi * 2 + z_lo), core: 2. Of those that a mesh axis runs over, the one named last changes fastest.
Arguments:
- checkpoints: bfloat16 [8, 2, 4096, 1024], P('section', None, ('dp', 'fsdp')), may hold values from -150 to 150
- cotangent: bfloat16 [2, 4096, 1024], P(None, ('dp', 'fsdp')), may hold values from -6 to 6
- weights: bfloat16 [8, 4, 1024, 1024], P('section', None, ('dp', 'fsdp')), may hold values from -6 to 6
- gains: bfloat16 [8, 1024], P('section', ('dp', 'fsdp')), may hold values from 0.099609375 to 1.8984375
- lengths: int32 [2, 31], replicated, may hold values from 1 to 256, 3840 in all within a row
Outputs:
- frame_grad: bfloat16 [8, 2, 4096, 1024], P('section', None, ('dp', 'fsdp'))
- weight_grad: float32 [8, 4, 1024, 1024], P('section', None, ('dp', 'fsdp'))
- gain_grad: float32 [8, 1024], P('section', ('dp', 'fsdp'))
Inputs may be any that keep to these rules, and one draw needn't show every extreme that they name: Each row of lengths adds up to 3840, and its longest utterance has exactly 256 frames; the last utterance, not listed, has 256 frames.
All inputs are finite; a program needn't handle non-finite values.
Results may differ from a plain program's by a relative error of at most 0.035.
The roundings to bfloat16 on the way count: a program that leaves them out, or rounds other values in their place, can miss the bound.
Values may be sent and summed in bfloat16 or wider, within the bound.
No kernel may reach another device: no remote copies, remote signals or barrier semaphores. Data moves between devices by JAX's collectives and lax.ppermute only.
A program may use at most 128 MiB of HBM per device.

v0:
```python
from functools import partial
import math

import jax
import jax.numpy as jnp
from jax import lax
from jax.experimental import pallas as pl
from jax.experimental.pallas import tpu as pltpu
from jax.sharding import PartitionSpec as P

HEAD = 128
BLOCK = 128
WIDTH = 1024
HEADS = WIDTH // HEAD
MICRO = 2
SCALE = 1.0 / math.sqrt(HEAD)
GROUP = ("dp", "fsdp")
EVERY = ("dp", "section", "fsdp")
MIB = 1024 * 1024
HEAD_ROWS = 16


def dot(left, right):
    return lax.dot_general(left, right, (((1,), (0,)), ((), ())), preferred_element_type=jnp.float32)


def dot_nt(left, right):
    return lax.dot_general(left, right, (((1,), (1,)), ((), ())), preferred_element_type=jnp.float32)


def dot_tn(left, right):
    return lax.dot_general(left, right, (((0,), (0,)), ((), ())), preferred_element_type=jnp.float32)


def shift(value, steps):
    count = lax.axis_size(GROUP)
    pairs = [(b, b + steps) for b in range(count) if 0 <= b + steps < count]
    return lax.ppermute(value, GROUP, pairs)


def hop(value, source, target, back):
    sections, rows = lax.axis_size("section"), lax.axis_size("fsdp")
    count = lax.axis_size(GROUP)

    def place(section, block):
        return (block // rows * sections + section) * rows + block % rows

    pairs = [(place(source, b), place(target, b - back)) for b in range(back, count)]
    return lax.ppermute(value, EVERY, pairs)


def group_dims():
    dp, fsdp = lax.axis_size("dp"), lax.axis_size("fsdp")
    planes = 2 if dp % 2 == 0 else 1
    return (planes, dp // planes, fsdp)


def turn(value, axis, steps):
    dims = group_dims()
    pairs = []
    for z in range(dims[0]):
        for y in range(dims[1]):
            for x in range(dims[2]):
                at = [z, y, x]
                to = list(at)
                to[axis] = (at[axis] + steps) % dims[axis]
                index = lambda p: (p[0] * dims[1] + p[1]) * dims[2] + p[2]
                pairs.append((index(at), index(to)))
    return lax.ppermute(value, GROUP, pairs)


def tie_kernel(*refs):
    del refs


def tie(value, *others):
    if not others:
        return value
    anywhere = pl.BlockSpec(memory_space=pl.ANY)
    return pl.pallas_call(
        tie_kernel,
        in_specs=[anywhere] * (1 + len(others)),
        out_specs=anywhere,
        out_shape=jax.ShapeDtypeStruct(value.shape, value.dtype),
        input_output_aliases={0: 0},
        name="tie",
    )(value, *others)


def ring(value, axis, head):
    size, half = group_dims()[axis], (value.shape[0] - head) // 2
    pieces = [(0, 0, value, head)]
    heads = [value[:head]]
    if size == 2:
        other = turn(value, axis, 1)
        pieces.append((1, 0, other, head))
        heads.append(other[:head])
    if size == 4:
        behind, ahead = turn(value, axis, 1), turn(value, axis, -1)
        up = turn(behind[: head + half], axis, 1)
        down = turn(ahead[head + half :], axis, -1)
        pieces += [(1, 0, ahead, head), (2, 0, up, head), (2, half, down, 0), (3, 0, behind, head)]
        heads += [ahead[:head], behind[:head], up[:head]]
    return pieces, sum(heads[1:], heads[0])


def gather_weights(shard, gain):
    share = shard.shape[1]
    value = jnp.concatenate([gain, shard.reshape(4 * share, WIDTH)])
    pair, gain = ring(value, 0, HEAD_ROWS)
    firsts = []
    for begin, axis in ((0, 1), (2 * share, 2)):
        parts = [piece[at + begin : at + begin + 2 * share] for _, _, piece, at in pair]
        head = HEAD_ROWS if begin == 0 else 0
        found, heads = ring(jnp.concatenate(([gain] if head else []) + parts), axis, head)
        gain = heads if head else gain
        rows = [piece[at:] for _, _, piece, at in found]
        firsts.append((rows, head))
    values = [jnp.concatenate(([gain] if head else []) + rows) for rows, head in firsts]
    values = [tie(values[0], values[1]), tie(values[1], values[0])]
    first, gain = ring(values[0], 2, HEAD_ROWS)
    second, _ = ring(values[1], 1, 0)
    return [first, second], gain


def normed(x, gain):
    as_float = x.astype(jnp.float32)
    rscale = lax.rsqrt(jnp.mean(as_float * as_float, axis=-1, keepdims=True) + 1e-06)
    return (as_float * rscale * gain).astype(jnp.bfloat16)


def forward_kernel(layout, dims, *refs):
    count = sum(len(pieces) for pieces in layout)
    spot, pieces, refs = refs[0], refs[1 : 1 + count], refs[1 + count :]
    l2, l1, own, r1, r2, gain, seg_col, seg_row = refs[:8]
    w_out, h_out, q_out, k_out, v_out, p_out, pt_out, o_out, a_out = refs[8:17]
    w, h5, q3, k5, v5, barred, sems = refs[17:]
    step = pl.program_id(0)
    planes, size_y, size_x = dims
    z, y, x = spot[0], spot[1], spot[2]

    def loads(pair):
        copies, offset = [], sum(len(pieces) for pieces in layout[:pair])
        share = WIDTH // (planes * size_y * size_x)
        for at, (place, first, begin, rows) in enumerate(layout[pair]):
            for row in range(rows // (2 * share)):
                one, plane = divmod(first // (2 * share) + row, planes)
                ahead_y, ahead_x = (one, place) if pair == 0 else (place, one)
                to = lax.rem(z + plane, planes) * size_y + lax.rem(y + ahead_y, size_y)
                to = to * size_x + lax.rem(x + ahead_x, size_x)
                to = pl.ds(pl.multiple_of(to * share, share), share)
                for m in range(2):
                    source = pieces[offset + at].at[pl.ds(begin + (2 * row + m) * share, share), :]
                    copies.append(
                        pltpu.make_async_copy(
                            source, w.at[2 * pair + m, to, :], sems.at[pair, len(copies)]
                        )
                    )
        return copies

    def store(pair):
        half = pl.ds(2 * pair, 2)
        return pltpu.make_async_copy(w.at[half], w_out.at[half], sems.at[2, pair])

    @pl.when(step == 0)
    def _():
        for copy in loads(0) + loads(1):
            copy.start()

    gain_row = gain[0:1, :]
    for at, part in enumerate((l2, l1, own, r1, r2)):
        h5[at * BLOCK : (at + 1) * BLOCK, :] = normed(part[0], gain_row)
    h_out[0] = h5[2 * BLOCK : 3 * BLOCK, :]

    @pl.when(step == 0)
    def _():
        for copy in loads(0):
            copy.wait()
        store(0).start()

    for n in range(0, WIDTH, 256):
        cols = slice(n, n + 256)
        q3[:, cols] = dot(h5[2 * BLOCK :, :], w[0, :, cols]).astype(jnp.bfloat16)
        k5[:, cols] = dot(h5[...], w[1, :, cols]).astype(jnp.bfloat16)

    @pl.when(step == 0)
    def _():
        for copy in loads(1):
            copy.wait()
        store(1).start()

    for n in range(0, WIDTH, 256):
        cols = slice(n, n + 256)
        v5[:, cols] = dot(h5[...], w[2, :, cols]).astype(jnp.bfloat16)
    q_out[0] = q3[...]
    k_out[0] = k5[: 3 * BLOCK, :]
    v_out[0] = v5[: 3 * BLOCK, :]
    for j in range(3):
        allowed = (
            seg_col[0, (j + 2) * BLOCK : (j + 3) * BLOCK, 0:1]
            == seg_row[0, 0:1, j * BLOCK : (j + 3) * BLOCK]
        )
        barred[j * BLOCK : (j + 1) * BLOCK, :] = jnp.where(allowed, 0.0, -1e30)
    for head in range(HEADS):
        cols = slice(head * HEAD, (head + 1) * HEAD)
        for j in range(3):
            rows = slice(j * BLOCK, (j + 1) * BLOCK)
            keys = slice(j * BLOCK, (j + 3) * BLOCK)
            score = dot_nt(q3[rows, cols], k5[keys, cols]) + barred[rows, :]
            top = jnp.max(score, axis=-1, keepdims=True)
            expo = jnp.exp((score - top) * SCALE)
            p = expo * (1.0 / jnp.sum(expo, axis=-1, keepdims=True))
            high = p.astype(jnp.bfloat16)
            low = (p - high.astype(jnp.float32)).astype(jnp.bfloat16)
            both = dot(jnp.concatenate([high, low]), v5[keys, cols])
            mixed = both[:BLOCK]
            o_out[0, rows, cols] = mixed + both[BLOCK:]
            if j == 0:
                p_out[0, head] = p
                a_out[0, :, cols] = mixed.astype(jnp.bfloat16)
            pt_out[0, head, :, rows] = p[:, (2 - j) * BLOCK : (3 - j) * BLOCK].T

    @pl.when(step == MICRO - 1)
    def _():
        store(0).wait()
        store(1).wait()


def forward(spot, pairs, parts, gain, seg_col, seg_row):
    anywhere = pl.BlockSpec(memory_space=pl.ANY)
    pieces = [piece for pair in pairs for _, _, piece, _ in pair]
    layout = [
        [(place, first, begin, piece.shape[0] - begin) for place, first, piece, begin in pair]
        for pair in pairs
    ]
    dims = group_dims()
    most = 2 * dims[0] * dims[1] * dims[2]

    def per_micro(shape):
        return pl.BlockSpec((1,) + shape, lambda m: (m,) + (0,) * len(shape))

    def whole(shape):
        return pl.BlockSpec(shape, lambda m: (0,) * len(shape), pipeline_mode=pl.Buffered(1))

    outs = [
        ((BLOCK, WIDTH), jnp.bfloat16),
        ((3 * BLOCK, WIDTH), jnp.bfloat16),
        ((3 * BLOCK, WIDTH), jnp.bfloat16),
        ((3 * BLOCK, WIDTH), jnp.bfloat16),
        ((HEADS, BLOCK, 3 * BLOCK), jnp.float32),
        ((HEADS, BLOCK, 3 * BLOCK), jnp.float32),
        ((3 * BLOCK, WIDTH), jnp.float32),
        ((BLOCK, WIDTH), jnp.bfloat16),
    ]
    return pl.pallas_call(
        partial(forward_kernel, layout, dims),
        grid=(MICRO,),
        in_specs=[pl.BlockSpec(memory_space=pltpu.SMEM)]
        + [anywhere] * len(pieces)
        + [per_micro((BLOCK, WIDTH))] * 5
        + [
            whole((8, WIDTH)),
            per_micro((5 * BLOCK, 1)),
            per_micro((1, 5 * BLOCK)),
        ],
        out_specs=[anywhere] + [per_micro(shape) for shape, _ in outs],
        out_shape=[jax.ShapeDtypeStruct((4, WIDTH, WIDTH), jnp.bfloat16)]
        + [jax.ShapeDtypeStruct((MICRO,) + shape, kind) for shape, kind in outs],
        scratch_shapes=[
            pltpu.VMEM((4, WIDTH, WIDTH), jnp.bfloat16),
            pltpu.VMEM((5 * BLOCK, WIDTH), jnp.bfloat16),
            pltpu.VMEM((3 * BLOCK, WIDTH), jnp.bfloat16),
            pltpu.VMEM((5 * BLOCK, WIDTH), jnp.bfloat16),
            pltpu.VMEM((5 * BLOCK, WIDTH), jnp.bfloat16),
            pltpu.VMEM((3 * BLOCK, 3 * BLOCK), jnp.float32),
            pltpu.SemaphoreType.DMA((3, most)),
        ],
        compiler_params=pltpu.CompilerParams(vmem_limit_bytes=44 * MIB),
        cost_estimate=pl.CostEstimate(
            flops=2 * 2 * 15 * BLOCK * WIDTH * WIDTH, bytes_accessed=28 << 20, transcendentals=0
        ),
        name="forward",
    )(spot, *pieces, *parts, gain, seg_col, seg_row)


def backward_kernel(micro, *refs):
    flag, g0, g1, g2, w, q_in, k_in, v_in, p_in, pt_in, o_in, x_in, gain_in = refs[:13]
    refs = refs[13:]
    frame_out, g_out, dq_out, dk_out, dv_out, gain_out = refs[:6]
    g, wv, q, k, v, p, pt, o, x, gain, da, dq, dk, dv, dh, frame, gain_sum, sems = refs[6:]

    @pl.when(flag[0] == 1)
    def _():
        def move(at, source, target):
            copy = pltpu.make_async_copy(source, target, sems.at[at])
            copy.start()
            return copy

        load_g = [
            move(at, part, g.at[pl.ds(at * BLOCK, BLOCK), :]) for at, part in enumerate((g0, g1, g2))
        ]
        load_wo = move(3, w.at[3], wv.at[3])
        load_o = move(4, o_in.at[micro], o)
        load_v = move(5, v_in.at[micro], v)
        load_p = move(6, p_in.at[micro], p)
        load_k = move(7, k_in.at[micro], k)
        load_pt = move(8, pt_in.at[micro], pt)
        load_q = move(9, q_in.at[micro], q)
        load_w = move(10, w.at[pl.ds(0, 3)], wv.at[pl.ds(0, 3)])
        load_x = move(11, x_in.at[micro], x)
        load_gain = move(12, gain_in, gain)
        for copy in load_g:
            copy.wait()
        load_wo.wait()
        store_g = move(13, g.at[pl.ds(0, BLOCK), :], g_out)
        for n in range(0, WIDTH, 256):
            cols = slice(n, n + 256)
            da[:, cols] = dot_nt(g[...], wv[3, cols, :]).astype(jnp.bfloat16)
        for copy in (load_o, load_v, load_p, load_k, load_pt, load_q):
            copy.wait()
        for head in range(HEADS):
            cols = slice(head * HEAD, (head + 1) * HEAD)
            da_h = da[:, cols]
            inner = jnp.sum(da_h.astype(jnp.float32) * o[:, cols], axis=-1, keepdims=True)
            dp = dot_nt(da_h[:BLOCK], v[:, cols])
            ds = (p[head] * (dp - inner[:BLOCK]) * SCALE).astype(jnp.bfloat16)
            dq[:, cols] = dot(ds, k[:, cols]).astype(jnp.bfloat16)
            inner_row = jnp.broadcast_to(inner, (3 * BLOCK, HEAD)).T
            p_t = pt[head]
            dp_t = dot_nt(v[2 * BLOCK :, cols], da_h)
            ds_t = (p_t * (dp_t - inner_row) * SCALE).astype(jnp.bfloat16)
            dk[:, cols] = dot(ds_t, q[:, cols]).astype(jnp.bfloat16)
            dv[:, cols] = dot(p_t.astype(jnp.bfloat16), da_h).astype(jnp.bfloat16)
        stores = [
            store_g,
            move(14, dq, dq_out),
            move(15, dk, dk_out),
            move(16, dv, dv_out),
        ]
        load_w.wait()
        for n in range(0, WIDTH, 256):
            cols = slice(n, n + 256)
            dh[:, cols] = (
                dot_nt(dq[...], wv[0, cols, :])
                + dot_nt(dk[...], wv[1, cols, :])
                + dot_nt(dv[...], wv[2, cols, :])
            )
        load_x.wait()
        load_gain.wait()
        as_float = x[...].astype(jnp.float32)
        rscale = lax.rsqrt(jnp.mean(as_float * as_float, axis=-1, keepdims=True) + 1e-06)
        d_normed = dh[...]
        scaled = gain[0:1, :] * d_normed
        cubic = rscale * rscale * rscale
        frame_f = (
            g[:BLOCK, :].astype(jnp.float32)
            + rscale * scaled
            - as_float * (cubic * jnp.mean(scaled * as_float, axis=-1, keepdims=True))
        )
        frame[...] = frame_f.astype(jnp.bfloat16)
        stores.append(move(17, frame, frame_out))
        term = jnp.sum(d_normed * as_float * rscale, axis=0, keepdims=True)
        gain_sum[...] = jnp.broadcast_to(term, (8, WIDTH))
        stores.append(move(18, gain_sum, gain_out))
        for copy in stores:
            copy.wait()


def in_place(value):
    return pltpu.with_memory_space_constraint(value, pltpu.HBM)


def backward(micro, flag, incoming, w, kept, x, gain):
    block = pltpu.HBM((BLOCK, WIDTH), jnp.bfloat16)
    outs = [block] * 5 + [pltpu.HBM((8, WIDTH), jnp.float32)]
    operands = [flag, *incoming] + [in_place(value) for value in (w, *kept, x, gain)]
    anywhere = pl.BlockSpec(memory_space=pl.ANY)
    in_hbm = pl.BlockSpec(memory_space=pltpu.HBM)
    bf16, f32 = jnp.bfloat16, jnp.float32
    scratch = [
        ((3 * BLOCK, WIDTH), bf16),
        ((4, WIDTH, WIDTH), bf16),
        ((3 * BLOCK, WIDTH), bf16),
        ((3 * BLOCK, WIDTH), bf16),
        ((3 * BLOCK, WIDTH), bf16),
        ((HEADS, BLOCK, 3 * BLOCK), f32),
        ((HEADS, BLOCK, 3 * BLOCK), f32),
        ((3 * BLOCK, WIDTH), f32),
        ((BLOCK, WIDTH), bf16),
        ((8, WIDTH), f32),
        ((3 * BLOCK, WIDTH), bf16),
        ((BLOCK, WIDTH), bf16),
        ((BLOCK, WIDTH), bf16),
        ((BLOCK, WIDTH), bf16),
        ((BLOCK, WIDTH), f32),
        ((BLOCK, WIDTH), bf16),
        ((8, WIDTH), f32),
    ]
    return pl.pallas_call(
        partial(backward_kernel, micro),
        in_specs=[pl.BlockSpec(memory_space=pltpu.SMEM)] + [anywhere] * (len(operands) - 1),
        out_specs=[in_hbm] * 6,
        out_shape=outs,
        scratch_shapes=[pltpu.VMEM(shape, kind) for shape, kind in scratch]
        + [pltpu.SemaphoreType.DMA((19,))],
        compiler_params=pltpu.CompilerParams(vmem_limit_bytes=48 * MIB),
        cost_estimate=pl.CostEstimate(
            flops=2 * 7 * BLOCK * WIDTH * WIDTH, bytes_accessed=16 << 20, transcendentals=0
        ),
        name="backward",
    )(*operands)


def ring_slots(size):
    if size == 4:
        return (2, 2, 2, 1, 1), {
            (0, 0): (0, 0), (1, 0): (0, 1),
            (0, 1): (3, 0), (1, 1): (1, 1),
            (0, 2): (1, 0), (1, 2): (2, 1),
            (0, 3): (2, 0), (1, 3): (4, 0),
        }
    return (2,) * size, {(m, f): (f, m) for m in range(2) for f in range(size)}


def ring_heads(size):
    return (1, 2) if size == 4 else (1,) * (size == 2)


def add(*values):
    return sum(value.astype(jnp.float32) for value in values)


def ring_sum(parts, axis, gain):
    size, head = group_dims()[axis], 0 if gain is None else HEAD_ROWS
    rows = parts[0].shape[0] // 2
    if size == 4:
        keep, up, down, late_up, late_down = parts
        up, down = turn(up, axis, 1), turn(down, axis, -1)
        late_up = add(late_up, up[head : head + rows]).astype(jnp.bfloat16)
        late_down = add(late_down, down[head + rows :]).astype(jnp.bfloat16)
        if head:
            late_up = jnp.concatenate([up[:head], late_up])
        late_up, late_down = turn(late_up, axis, 1), turn(late_down, axis, -1)
        total = [
            add(keep[:rows], late_up[head:], down[head : head + rows]),
            add(keep[rows:], up[head + rows :], late_down),
        ]
        if head:
            gain = add(gain, up[:head], down[:head], late_up[:head])
        return jnp.stack(total), gain
    if size == 2:
        other = turn(parts[1], axis, 1)
        if head:
            gain = add(gain, other[:head])
        return add(parts[0], other[head:]).reshape(2, rows, WIDTH), gain
    return parts[0].astype(jnp.float32).reshape(2, rows, WIDTH), gain


def collect_kernel(sections, dims, counts, *refs):
    place, spot, h_in, a_in = refs[:4]
    kept = refs[4 : 4 + 12 * sections]
    refs = refs[4 + 12 * sections :]
    frame_out, gain_out, outs = refs[0], refs[1], refs[2 : 2 + sum(counts)]
    left, right, term, frame, gain, gain_head, sems, out_sems = refs[2 + sum(counts) :]
    planes, size_y, size_x = dims
    share = WIDTH // (planes * size_y * size_x)
    own_y, own_x = spot[1], spot[2]
    names = ("frame", "g", "dq", "dk", "dv", "gain")

    def copies(at):
        found = []
        for micro in range(MICRO):
            results = dict(zip(names, kept[(at * MICRO + micro) * 6 : (at * MICRO + micro + 1) * 6]))
            rows = pl.ds(micro * BLOCK, BLOCK)
            pairs = [(results[name], right.at[n, rows]) for n, name in enumerate(("dq", "dk", "dv", "g"))]
            pairs += [(results["frame"], frame.at[micro]), (results["gain"], gain.at[micro])]
            pairs += [(h_in.at[micro], left.at[0, rows]), (a_in.at[micro], left.at[1, rows])]
            found += [
                pltpu.make_async_copy(source, target, sems.at[micro, n])
                for n, (source, target) in enumerate(pairs)
            ]
        return found

    for at in range(sections):

        @pl.when(place[0] == at)
        def _(at=at):
            started = copies(at)
            for copy in started:
                copy.start()
            for copy in started:
                copy.wait()

    frame_copy = pltpu.make_async_copy(frame, frame_out, out_sems.at[4, 0])
    frame_copy.start()
    gain_term = (gain[0, 0:1, :] + gain[1, 0:1, :]).astype(jnp.bfloat16)
    gain_head[...] = jnp.broadcast_to(gain_term, (HEAD_ROWS, WIDTH))
    started = [frame_copy]
    heads = [gain_out] + [outs[at].at[pl.ds(0, HEAD_ROWS), :] for at in ring_heads(size_x)]
    for at, target in enumerate(heads):
        copy = pltpu.make_async_copy(gain_head, target, out_sems.at[4, 1 + at])
        copy.start()
        started.append(copy)
    for m in range(4):
        pair = m // 2
        first_size, second_size = (size_x, size_y) if pair == 0 else (size_y, size_x)
        _, slots = ring_slots(first_size)
        arrays = outs[: counts[0]] if pair == 0 else outs[counts[0] :]
        factor = left[1 if m == 3 else 0]
        for n in range(0, WIDTH, 256):
            cols = slice(n, n + 256)
            term[m, :, cols] = dot_tn(factor, right[m, :, cols]).astype(jnp.bfloat16)
        number = 0
        for f in range(first_size):
            array, row = slots[m % 2, f]
            for r in range(second_size):
                ahead_x, ahead_y = (f, r) if pair == 0 else (r, f)
                column = lax.rem(own_y + ahead_y, size_y) * size_x + lax.rem(own_x + ahead_x, size_x)
                for plane in range(planes):
                    at = (plane * size_y * size_x + column) * share
                    to = ((row * second_size + r) * planes + plane) * share
                    if pair == 0 and array in ring_heads(first_size):
                        to += HEAD_ROWS
                    copy = pltpu.make_async_copy(
                        term.at[m, pl.ds(pl.multiple_of(at, share), share), :],
                        arrays[array].at[pl.ds(to, share), :],
                        out_sems.at[m, number],
                    )
                    copy.start()
                    started.append(copy)
                    number += 1
    for copy in started:
        copy.wait()


def collect(section, spot, h, a, kept):
    dims, sections = group_dims(), len(kept)
    planes, size_y, size_x = dims
    total = planes * size_y * size_x
    share = WIDTH // total
    anywhere = pl.BlockSpec(memory_space=pl.ANY)
    in_hbm = pl.BlockSpec(memory_space=pltpu.HBM)
    smem = pl.BlockSpec(memory_space=pltpu.SMEM)
    shapes, counts = [], []
    for first_size, second_size in ((size_x, size_y), (size_y, size_x)):
        rows, _ = ring_slots(first_size)
        counts.append(len(rows))
        for at, n in enumerate(rows):
            n = n * second_size * planes * share
            if len(counts) == 1 and at in ring_heads(first_size):
                n += HEAD_ROWS
            shapes.append(jax.ShapeDtypeStruct((n, WIDTH), jnp.bfloat16))
    operands = [in_place(result) for both in kept for results in both for result in results]
    outs = pl.pallas_call(
        partial(collect_kernel, sections, dims, counts),
        in_specs=[smem, smem] + [anywhere] * (2 + len(operands)),
        out_specs=[in_hbm] * (2 + len(shapes)),
        out_shape=[
            jax.ShapeDtypeStruct((MICRO, BLOCK, WIDTH), jnp.bfloat16),
            jax.ShapeDtypeStruct((HEAD_ROWS, WIDTH), jnp.bfloat16),
        ]
        + shapes,
        scratch_shapes=[
            pltpu.VMEM((2, MICRO * BLOCK, WIDTH), jnp.bfloat16),
            pltpu.VMEM((4, MICRO * BLOCK, WIDTH), jnp.bfloat16),
            pltpu.VMEM((4, WIDTH, WIDTH), jnp.bfloat16),
            pltpu.VMEM((MICRO, BLOCK, WIDTH), jnp.bfloat16),
            pltpu.VMEM((MICRO, 8, WIDTH), jnp.float32),
            pltpu.VMEM((HEAD_ROWS, WIDTH), jnp.bfloat16),
            pltpu.SemaphoreType.DMA((MICRO, 8)),
            pltpu.SemaphoreType.DMA((5, max(total, 4))),
        ],
        compiler_params=pltpu.CompilerParams(vmem_limit_bytes=48 * MIB),
        cost_estimate=pl.CostEstimate(
            flops=2 * 8 * BLOCK * WIDTH * WIDTH, bytes_accessed=14 << 20, transcendentals=0
        ),
        name="collect",
    )(section, spot, h, a, *operands)
    frame, gain = outs[:2]
    return frame, gain, [outs[2 : 2 + counts[0]], outs[2 + counts[0] :]]


def sum_terms(parts, gain, plane):
    dims, totals = group_dims(), []
    for pair, (first, second) in zip(parts, ((2, 1), (1, 2))):
        own = gain if first == 2 else None
        value, own = ring_sum(pair, first, own)
        value = value.astype(jnp.bfloat16).reshape(2, dims[second], -1, WIDTH)
        rows, slots = ring_slots(dims[second])
        arrays = [[None] * n for n in rows]
        for (m, f), (array, row) in slots.items():
            arrays[array][row] = value[m, f]
        if own is not None:
            own = own.astype(jnp.bfloat16)
            for array in ring_heads(dims[second]):
                arrays[array].insert(0, own)
        value, own = ring_sum([jnp.concatenate(array) for array in arrays], second, own)
        totals.append(value)
        gain = gain if own is None else own
    value = jnp.concatenate(totals)
    if dims[0] == 1:
        return value, gain
    share = value.shape[1] // 2
    value = value.reshape(4, 2, share, WIDTH)
    other = lax.dynamic_index_in_dim(value, 1 - plane, 1, keepdims=False).astype(jnp.bfloat16)
    own = lax.dynamic_index_in_dim(value, plane, 1, keepdims=False)
    other = jnp.concatenate([gain.astype(jnp.bfloat16), other.reshape(4 * share, WIDTH)])
    other = turn(other, 0, 1)
    return add(own, other[HEAD_ROWS:].reshape(own.shape)), add(gain, other[:HEAD_ROWS])


def segments(lengths, block):
    bounds = jnp.cumsum(lengths, axis=1)
    total = lax.axis_size(GROUP) * BLOCK
    places = (block - 2) * BLOCK + jnp.arange(5 * BLOCK, dtype=jnp.int32)
    counted = jnp.sum((places[None, :, None] >= bounds[:, None, :]).astype(jnp.int32), axis=2)
    return jnp.where(places < 0, -1, jnp.where(places >= total, -2, counted))


def body(checkpoints, cotangent, weights, gains, lengths):
    sections, section = lax.axis_size("section"), lax.axis_index("section")
    block = lax.axis_index(GROUP)
    share = gains.shape[1]

    planes, size_y, _ = group_dims()
    dp = lax.axis_index("dp")
    spot = jnp.stack([dp // size_y, dp % size_y, lax.axis_index("fsdp")]).astype(jnp.int32)
    spread = lax.dynamic_update_slice(
        jnp.zeros((HEAD_ROWS, WIDTH), jnp.bfloat16), gains, (0, block * share)
    )
    pairs, gain = gather_weights(weights[0], spread)
    gain = jnp.broadcast_to(gain[0:1].astype(jnp.float32), (8, WIDTH))

    x = checkpoints[0]
    left, right = shift(x, 1), shift(x, -1)
    parts = (shift(left, 1), left, x, right, shift(right, -1))
    source = max(sections - 3, 0)
    cot = (cotangent, hop(cotangent, source, sections - 1, 1), hop(cotangent, source, sections - 1, 2))

    segs = segments(lengths, block)
    gathered, h, q, k, v, p, pt, o, a = forward(
        spot, pairs, parts, gain, segs[:, :, None], segs[:, None, :]
    )
    kept = (q, k, v, p, pt, o)

    kept_grads = [[None] * MICRO for _ in range(sections)]
    incoming = [[part[micro] for part in cot] for micro in range(MICRO)]
    for at in range(sections - 1, -1, -1):
        flag = (section == at).astype(jnp.int32).reshape(1)
        for micro in range(MICRO):
            grads = list(backward(micro, flag, incoming[micro], gathered, kept, x, gain))
            if at > 0:
                before = incoming[micro - 1] if micro > 0 else []
                if at % 2 == 1:
                    grads[0] = tie(grads[0], *before)
                    incoming[micro] = [hop(grads[0], at, at - 1, back) for back in range(3)]
                else:
                    grads[0] = tie(grads[0], *before[:1])
                    own = tie(hop(grads[0], at, at - 1, 0), *before[1:])
                    incoming[micro] = [own] + [hop(own, at - 1, at - 1, back) for back in (1, 2)]
            kept_grads[at][micro] = grads

    place = section.astype(jnp.int32).reshape(1)
    frame, gain_part, parts = collect(place, spot, h, a, kept_grads)
    weight_part, gain_sum = sum_terms(parts, gain_part, spot[0])
    gain_sum = lax.dynamic_slice(gain_sum, (0, block * share), (1, share))
    return (frame[None], weight_part[None], gain_sum)


def solution(mesh):
    placed = (
        P("section", None, ("dp", "fsdp"), None),
        P(None, ("dp", "fsdp"), None),
        P("section", None, ("dp", "fsdp"), None),
        P("section", ("dp", "fsdp")),
        P(),
    )
    return jax.shard_map(
        body,
        mesh=mesh,
        in_specs=placed,
        out_specs=(
            P("section", None, ("dp", "fsdp"), None),
            P("section", None, ("dp", "fsdp"), None),
            P("section", ("dp", "fsdp")),
        ),
        check_vma=False,
    )
```

profile of v0, /device:TPU:6, one launch (start us, length us, event | category | flops | bytes accessed | tf_op | source)
XLA Modules:
  0.0 543.8 jit_solution(671272518665307328)
XLA Ops:
  5.5 6.0 %collective-permute-done = bf16[144,1024]{1,0:T(8,128)(2,1)S(1)} collective-permute-done((bf16[144,1024]{1,0:T(8,128)(2,1)S(1)}, bf16[144,1024]{1,0:T(8,128)(2,1)S(1)}, u32[]{:S(2)}, u32[]{:S(2)}) %collective-permute-start) | collective-permute-done | bytes 294944 | tf_op jit(solution)/shard_map/ppermute | solution.py:69
  15.2 6.1 %collective-permute-done.2 = bf16[144,1024]{1,0:T(8,128)(2,1)S(1)} collective-permute-done((bf16[144,1024]{1,0:T(8,128)(2,1)S(1)}, bf16[144,1024]{1,0:T(8,128)(2,1)S(1)}, u32[]{:S(2)}, u32[]{:S(2)}) %collective-permute-start.2) | collective-permute-done | bytes 294944 | tf_op jit(solution)/shard_map/ppermute | solution.py:69
  31.4 5.2 collective-permute-done.6
  41.9 3.8 collective-permute-done.8
  56.1 16.6 %collective-permute-done.10.refs_5_ = bf16[528,1024]{1,0:T(8,128)(2,1)} collective-permute-done((bf16[528,1024]{1,0:T(8,128)(2,1)}, bf16[528,1024]{1,0:T(8,128)(2,1)}, u32[]{:S(2)}, u32[]{:S(2)}) %collective-permute-start.10) | collective-permute-done | bytes 1081376 | tf_op jit(solution)/shard_map/ppermute | solution.py:69
  86.1 4.9 collective-permute-start.18
  106.6 5.5 %collective-permute-done.16.refs_9_ = bf16[256,1024]{1,0:T(8,128)(2,1)S(1)} collective-permute-done((bf16[256,1024]{1,0:T(8,128)(2,1)S(1)}, bf16[256,1024]{1,0:T(8,128)(2,1)S(1)}, u32[]{:S(2)}, u32[]{:S(2)}) %collective-permute-start.16) | collective-permute-done | bytes 524320 | tf_op jit(solution)/shard_map/ppermute | solution.py:69
  113.5 40.8 %forward.1 = (bf16[4,1024,1024]{2,1,0:T(8,128)(2,1)}, bf16[2,128,1024]{2,1,0:T(8,128)(2,1)S(1)}, bf16[2,384,1024]{2,1,0:T(8,128)(2,1)}, bf16[2,384,1024]{2,1,0:T...) custom-call(s32[3]{0:T(128)S(1)} %pad_add_fusion.refs_0_.refs_1_, ...), custom_call_target="tpu_custom_call" | custom-call | flops 8053063680 | bytes 29360128 | tf_op jit(solution)/shard_map/forward/pallas_call | solution.py:255
  211.6 176.6 %collective-permute-done.41.refs_1_ = bf16[128,1024]{1,0:T(8,128)(2,1)S(1)} collective-permute-done((bf16[128,1024]{1,0:T(8,128)(2,1)}, bf16[128,1024]{1,0:T(8,128)(2,1)S(1)}, u32[]{:S(2)}, u32[]{:S(2)}) %collective-permute-start.41) | collective-permute-done | bytes 262176 | tf_op jit(solution)/shard_map/ppermute | solution.py:49
  388.2 7.8 %collective-permute-done.42.refs_2_ = bf16[128,1024]{1,0:T(8,128)(2,1)S(1)} collective-permute-done((bf16[128,1024]{1,0:T(8,128)(2,1)}, bf16[128,1024]{1,0:T(8,128)(2,1)S(1)}, u32[]{:S(2)}, u32[]{:S(2)}) %collective-permute-start.42) | collective-permute-done | bytes 262176 | tf_op jit(solution)/shard_map/ppermute | solution.py:49
  406.5 10.3 %backward.23 = (bf16[128,1024]{1,0:T(8,128)(2,1)}, bf16[128,1024]{1,0:T(8,128)(2,1)}, bf16[128,1024]{1,0:T(8,128)(2,1)}, bf16[128,1024]{1,0:T(8,128)(2,1)}, bf16...) custom-call(s32[1]{0:T(128)} %bitcast.10.refs_0_, bf16[128,1024]{1,0:T(8,128)(2,1)S(1)} %copy-done.14, ...), custom_call_target="tpu_custom_call" | custom-call | flops 1879048192 | bytes 16777216 | tf_op jit(solution)/shard_map/backward/pallas_call | solution.py:399
  416.9 10.2 %backward.31 = (bf16[128,1024]{1,0:T(8,128)(2,1)}, bf16[128,1024]{1,0:T(8,128)(2,1)}, bf16[128,1024]{1,0:T(8,128)(2,1)}, bf16[128,1024]{1,0:T(8,128)(2,1)}, bf16...) custom-call(s32[1]{0:T(128)} %bitcast.10.refs_0_, bf16[128,1024]{1,0:T(8,128)(2,1)S(1)} %collective-permute-done.62.refs_1_, ...), custom_call_target="tpu_custom_call" | custom-call | flops 1879048192 | bytes 16777216 | tf_op jit(solution)/shard_map/backward/pallas_call | solution.py:399
  427.1 13.9 %collect.1 = (bf16[2,128,1024]{2,1,0:T(8,128)(2,1)}, bf16[16,1024]{1,0:T(8,128)(2,1)S(1)}, bf16[512,1024]{1,0:T(8,128)(2,1)S(1)}, bf16[528,1024]{1,0:T(8,128)(2,...) custom-call(s32[1]{0:T(128)} %bitcast.refs_0_, ...), custom_call_target="tpu_custom_call" | custom-call | flops 2147483648 | bytes 14680064 | tf_op jit(solution)/shard_map/collect/pallas_call | solution.py:554
  441.0 18.3 %collective-permute-start.75 = (bf16[512,1024]{1,0:T(8,128)(2,1)}, bf16[512,1024]{1,0:T(8,128)(2,1)S(1)}, u32[]{:S(2)}, u32[]{:S(2)}) collective-permute-start(bf16[512,1024]{1,0:T(8,128)(2,1)} %get-tuple-element.235), channel_id=1, source_target_pairs={{0,96},{1,97},{2,98},{3,99},{32,0},{33,1},{34,2},{35,3},{64,32},{6... | collective-permute-start | bytes 3145736 | tf_op jit(solution)/shard_map/ppermute | solution.py:69
  459.3 18.2 %collective-permute-done.75 = bf16[512,1024]{1,0:T(8,128)(2,1)S(1)} collective-permute-done((bf16[512,1024]{1,0:T(8,128)(2,1)}, bf16[512,1024]{1,0:T(8,128)(2,1)S(1)}, u32[]{:S(2)}, u32[]{:S(2)}) %collective-permute-start.75) | collective-permute-done | bytes 1048608 | tf_op jit(solution)/shard_map/ppermute | solution.py:69
  477.7 3.7 collective-permute-start.76
  488.1 4.0 collective-permute-done.74
  496.4 7.3 %collective-permute-done.67 = bf16[528,1024]{1,0:T(8,128)(2,1)S(1)} collective-permute-done((bf16[528,1024]{1,0:T(8,128)(2,1)S(1)}, bf16[528,1024]{1,0:T(8,128)(2,1)S(1)}, u32[]{:S(2)}, u32[]{:S(2)}) %collective-permute-start.67) | collective-permute-done | bytes 1081376 | tf_op jit(solution)/shard_map/ppermute | solution.py:69
  508.3 6.4 %collective-permute-done.68 = bf16[256,1024]{1,0:T(8,128)(2,1)S(1)} collective-permute-done((bf16[256,1024]{1,0:T(8,128)(2,1)S(1)}, bf16[256,1024]{1,0:T(8,128)(2,1)S(1)}, u32[]{:S(2)}, u32[]{:S(2)}) %collective-permute-start.68) | collective-permute-done | bytes 524320 | tf_op jit(solution)/shard_map/ppermute | solution.py:69
  516.4 3.3 collective-permute-start.71
  519.6 3.4 collective-permute-done.69
  523.9 5.8 %collective-permute-done.70 = bf16[80,1024]{1,0:T(8,128)(2,1)S(1)} collective-permute-done((bf16[80,1024]{1,0:T(8,128)(2,1)S(1)}, bf16[80,1024]{1,0:T(8,128)(2,1)S(1)}, u32[]{:S(2)}, u32[]{:S(2)}) %collective-permute-start.70) | collective-permute-done | bytes 163872 | tf_op jit(solution)/shard_map/ppermute | solution.py:69
  529.9 4.9 collective-permute-done.72
  535.3 6.6 %collective-permute-done.81 = bf16[144,1024]{1,0:T(8,128)(2,1)S(1)} collective-permute-done((bf16[144,1024]{1,0:T(8,128)(2,1)S(1)}, bf16[144,1024]{1,0:T(8,128)(2,1)S(1)}, u32[]{:S(2)}, u32[]{:S(2)}) %collective-permute-start.81) | collective-permute-done | bytes 294944 | tf_op jit(solution)/shard_map/ppermute | solution.py:69
  (373 shorter events, 151.4 us)
Async XLA Ops:
  47.1 25.6 %collective-permute-start.10 = (bf16[528,1024]{1,0:T(8,128)(2,1)}, bf16[528,1024]{1,0:T(8,128)(2,1)}, u32[]{:S(2)}, u32[]{:S(2)}) collective-permute-start(bf16[528,1024]{1,0:T(8,128)(2,1)} %tie.12.refs_1_), channel_id=1, source_target_pairs={{0,1},{1,2},{2,3},{3,0},{32,33},{33,34},{34,35},{35,32},{64,65},{6... | collective-permute-start | bytes 3244040 | tf_op jit(solution)/shard_map/ppermute | solution.py:69
  48.3 32.3 %collective-permute-start.14 = (bf16[512,1024]{1,0:T(8,128)(2,1)S(1)}, bf16[512,1024]{1,0:T(8,128)(2,1)S(1)}, u32[]{:S(2)}, u32[]{:S(2)}) collective-permute-start(bf16[512,1024]{1,0:T(8,128)(2,1)S(1)} %copy-done.2), channel_id=1, source_target_pairs={{0,32},{1,33},{2,34},{3,35},{32,64},{33,65},{34,66},{35,67},{64,96... | collective-permute-start | bytes 3145736 | tf_op jit(solution)/shard_map/ppermute | solution.py:69
  48.3 33.7 %collective-permute-start.13 = (bf16[512,1024]{1,0:T(8,128)(2,1)S(1)}, bf16[512,1024]{1,0:T(8,128)(2,1)}, u32[]{:S(2)}, u32[]{:S(2)}) collective-permute-start(bf16[512,1024]{1,0:T(8,128)(2,1)S(1)} %copy-done.2), channel_id=1, source_target_pairs={{0,96},{1,97},{2,98},{3,99},{32,0},{33,1},{34,2},{35,3},{64,32},{6... | collective-permute-start | bytes 3145736 | tf_op jit(solution)/shard_map/ppermute | solution.py:69
  51.5 27.6 %collective-permute-start.17 = (bf16[2,128,1024]{2,1,0:T(8,128)(2,1)S(1)}, bf16[2,128,1024]{2,1,0:T(8,128)(2,1)S(1)}, u32[]{:S(2)}, u32[]{:S(2)}) collective-permute-start(bf16[2,128,1024]{2,1,0:T(8,128)(2,1)S(1)} %bitcast.124), channel_id=1, source_target_pairs={{0,1},{1,2},{2,3},{3,32},{32,33},{33,34},{34,35},{35,64},{64,65},{... | collective-permute-start | bytes 1572872 | tf_op jit(solution)/shard_map/ppermute | solution.py:38
  53.5 37.5 %collective-permute-start.9 = (bf16[528,1024]{1,0:T(8,128)(2,1)}, bf16[528,1024]{1,0:T(8,128)(2,1)}, u32[]{:S(2)}, u32[]{:S(2)}) collective-permute-start(bf16[528,1024]{1,0:T(8,128)(2,1)} %tie.12.refs_1_), channel_id=1, source_target_pairs={{0,3},{1,0},{2,1},{3,2},{32,35},{33,32},{34,33},{35,34},{64,67},{6... | collective-permute-start | bytes 3244040 | tf_op jit(solution)/shard_map/ppermute | solution.py:69
  79.1 14.9 %collective-permute-start.22 = (bf16[2,128,1024]{2,1,0:T(8,128)(2,1)}, bf16[2,128,1024]{2,1,0:T(8,128)(2,1)}, u32[]{:S(2)}, u32[]{:S(2)}) collective-permute-start(bf16[2,128,1024]{2,1,0:T(8,128)(2,1)} %param.6), channel_id=1, source_target_pairs={{22,28},{23,29},{52,30},{53,31},{54,60},{55,61},{84,62},{85,63},{8... | collective-permute-start | bytes 1572872 | tf_op jit(solution)/shard_map/ppermute | solution.py:49
  80.6 16.1 %collective-permute-start.21 = (bf16[2,128,1024]{2,1,0:T(8,128)(2,1)}, bf16[2,128,1024]{2,1,0:T(8,128)(2,1)}, u32[]{:S(2)}, u32[]{:S(2)}) collective-permute-start(bf16[2,128,1024]{2,1,0:T(8,128)(2,1)} %param.6), channel_id=1, source_target_pairs={{21,28},{22,29},{23,30},{52,31},{53,60},{54,61},{55,62},{84,63},{8... | collective-permute-start | bytes 1572872 | tf_op jit(solution)/shard_map/ppermute | solution.py:49
  82.1 15.3 %collective-permute-start.11 = (bf16[272,1024]{1,0:T(8,128)(2,1)}, bf16[272,1024]{1,0:T(8,128)(2,1)}, u32[]{:S(2)}, u32[]{:S(2)}) collective-permute-start(bf16[272,1024]{1,0:T(8,128)(2,1)} %slice.348), channel_id=1, source_target_pairs={{0,1},{1,2},{2,3},{3,0},{32,33},{33,34},{34,35},{35,32},{64,65},{6... | collective-permute-start | bytes 1671176 | tf_op jit(solution)/shard_map/ppermute | solution.py:69
  86.1 17.5 %collective-permute-start.18 = (bf16[2,128,1024]{2,1,0:T(8,128)(2,1)S(1)}, bf16[2,128,1024]{2,1,0:T(8,128)(2,1)S(1)}, u32[]{:S(2)}, u32[]{:S(2)}) collective-permute-start(bf16[2,128,1024]{2,1,0:T(8,128)(2,1)S(1)} %collective-permute-done.17.refs_12_), channel_id=1, source_target_pairs={{0,1},{1,2},{2,3},{3,32},{32,33},{33,34},{34,35},{35,64},{64,65},{... | collective-permute-start | bytes 1572872 | tf_op jit(solution)/shard_map/ppermute | solution.py:38
  91.0 15.6 %collective-permute-start.20 = (bf16[2,128,1024]{2,1,0:T(8,128)(2,1)}, bf16[2,128,1024]{2,1,0:T(8,128)(2,1)S(1)}, u32[]{:S(2)}, u32[]{:S(2)}) collective-permute-start(bf16[2,128,1024]{2,1,0:T(8,128)(2,1)} %collective-permute-done.19.refs_14_), channel_id=1, source_target_pairs={{1,0},{2,1},{3,2},{32,3},{33,32},{34,33},{35,34},{64,35},{65,64},{... | collective-permute-start | bytes 1572872 | tf_op jit(solution)/shard_map/ppermute | solution.py:38
  96.7 15.4 %collective-permute-start.16 = (bf16[256,1024]{1,0:T(8,128)(2,1)S(1)}, bf16[256,1024]{1,0:T(8,128)(2,1)S(1)}, u32[]{:S(2)}, u32[]{:S(2)}) collective-permute-start(bf16[256,1024]{1,0:T(8,128)(2,1)S(1)} %slice.351), channel_id=1, source_target_pairs={{0,96},{1,97},{2,98},{3,99},{32,0},{33,1},{34,2},{35,3},{64,32},{6... | collective-permute-start | bytes 1572872 | tf_op jit(solution)/shard_map/ppermute | solution.py:69
  97.4 16.1 %collective-permute-start.12 = (bf16[256,1024]{1,0:T(8,128)(2,1)S(1)}, bf16[256,1024]{1,0:T(8,128)(2,1)S(1)}, u32[]{:S(2)}, u32[]{:S(2)}) collective-permute-start(bf16[256,1024]{1,0:T(8,128)(2,1)S(1)} %slice.349), channel_id=1, source_target_pairs={{0,3},{1,0},{2,1},{3,2},{32,35},{33,32},{34,33},{35,34},{64,67},{6... | collective-permute-start | bytes 1572872 | tf_op jit(solution)/shard_map/ppermute | solution.py:69
  207.5 180.7 %collective-permute-start.41 = (bf16[128,1024]{1,0:T(8,128)(2,1)}, bf16[128,1024]{1,0:T(8,128)(2,1)S(1)}, u32[]{:S(2)}, u32[]{:S(2)}) collective-permute-start(bf16[128,1024]{1,0:T(8,128)(2,1)} %get-tuple-element.135.refs_16_), channel_id=1, source_target_pairs={{4,0},{5,1},{6,2},{7,3},{36,32},{37,33},{38,34},{39,35},{68,64},{6... | collective-permute-start | bytes 786440 | tf_op jit(solution)/shard_map/ppermute | solution.py:49
  208.8 187.2 %collective-permute-start.42 = (bf16[128,1024]{1,0:T(8,128)(2,1)}, bf16[128,1024]{1,0:T(8,128)(2,1)S(1)}, u32[]{:S(2)}, u32[]{:S(2)}) collective-permute-start(bf16[128,1024]{1,0:T(8,128)(2,1)} %get-tuple-element.135.refs_16_), channel_id=1, source_target_pairs={{5,0},{6,1},{7,2},{36,3},{37,32},{38,33},{39,34},{68,35},{69,64},{... | collective-permute-start | bytes 786440 | tf_op jit(solution)/shard_map/ppermute | solution.py:49
  210.1 189.0 %collective-permute-start.43 = (bf16[128,1024]{1,0:T(8,128)(2,1)}, bf16[128,1024]{1,0:T(8,128)(2,1)S(1)}, u32[]{:S(2)}, u32[]{:S(2)}) collective-permute-start(bf16[128,1024]{1,0:T(8,128)(2,1)} %get-tuple-element.135.refs_16_), channel_id=1, source_target_pairs={{6,0},{7,1},{36,2},{37,3},{38,32},{39,33},{68,34},{69,35},{70,64},... | collective-permute-start | bytes 786440 | tf_op jit(solution)/shard_map/ppermute | solution.py:49
  399.8 17.1 %collective-permute-start.62 = (bf16[128,1024]{1,0:T(8,128)(2,1)}, bf16[128,1024]{1,0:T(8,128)(2,1)S(1)}, u32[]{:S(2)}, u32[]{:S(2)}) collective-permute-start(bf16[128,1024]{1,0:T(8,128)(2,1)} %tie.23.refs_22_), channel_id=1, source_target_pairs={{4,0},{5,1},{6,2},{7,3},{36,32},{37,33},{38,34},{39,35},{68,64},{6... | collective-permute-start | bytes 786440 | tf_op jit(solution)/shard_map/ppermute | solution.py:49
  401.1 15.8 %collective-permute-start.63 = (bf16[128,1024]{1,0:T(8,128)(2,1)}, bf16[128,1024]{1,0:T(8,128)(2,1)S(1)}, u32[]{:S(2)}, u32[]{:S(2)}) collective-permute-start(bf16[128,1024]{1,0:T(8,128)(2,1)} %tie.23.refs_22_), channel_id=1, source_target_pairs={{5,0},{6,1},{7,2},{36,3},{37,32},{38,33},{39,34},{68,35},{69,64},{... | collective-permute-start | bytes 786440 | tf_op jit(solution)/shard_map/ppermute | solution.py:49
  402.4 14.5 %collective-permute-start.64 = (bf16[128,1024]{1,0:T(8,128)(2,1)}, bf16[128,1024]{1,0:T(8,128)(2,1)S(1)}, u32[]{:S(2)}, u32[]{:S(2)}) collective-permute-start(bf16[128,1024]{1,0:T(8,128)(2,1)} %tie.23.refs_22_), channel_id=1, source_target_pairs={{6,0},{7,1},{36,2},{37,3},{38,32},{39,33},{68,34},{69,35},{70,64},... | collective-permute-start | bytes 786440 | tf_op jit(solution)/shard_map/ppermute | solution.py:49
  441.0 36.5 %collective-permute-start.75 = (bf16[512,1024]{1,0:T(8,128)(2,1)}, bf16[512,1024]{1,0:T(8,128)(2,1)S(1)}, u32[]{:S(2)}, u32[]{:S(2)}) collective-permute-start(bf16[512,1024]{1,0:T(8,128)(2,1)} %get-tuple-element.235), channel_id=1, source_target_pairs={{0,96},{1,97},{2,98},{3,99},{32,0},{33,1},{34,2},{35,3},{64,32},{6... | collective-permute-start | bytes 3145736 | tf_op jit(solution)/shard_map/ppermute | solution.py:69
  459.2 22.1 %collective-permute-start.73 = (bf16[512,1024]{1,0:T(8,128)(2,1)}, bf16[512,1024]{1,0:T(8,128)(2,1)S(1)}, u32[]{:S(2)}, u32[]{:S(2)}) collective-permute-start(bf16[512,1024]{1,0:T(8,128)(2,1)} %get-tuple-element.234), channel_id=1, source_target_pairs={{0,32},{1,33},{2,34},{3,35},{32,64},{33,65},{34,66},{35,67},{64,96... | collective-permute-start | bytes 3145736 | tf_op jit(solution)/shard_map/ppermute | solution.py:69
  459.2 23.6 %collective-permute-start.65 = (bf16[528,1024]{1,0:T(8,128)(2,1)}, bf16[528,1024]{1,0:T(8,128)(2,1)S(1)}, u32[]{:S(2)}, u32[]{:S(2)}) collective-permute-start(bf16[528,1024]{1,0:T(8,128)(2,1)} %get-tuple-element.227), channel_id=1, source_target_pairs={{0,1},{1,2},{2,3},{3,0},{32,33},{33,34},{34,35},{35,32},{64,65},{6... | collective-permute-start | bytes 3244040 | tf_op jit(solution)/shard_map/ppermute | solution.py:69
  481.7 22.0 %collective-permute-start.67 = (bf16[528,1024]{1,0:T(8,128)(2,1)S(1)}, bf16[528,1024]{1,0:T(8,128)(2,1)S(1)}, u32[]{:S(2)}, u32[]{:S(2)}) collective-permute-start(bf16[528,1024]{1,0:T(8,128)(2,1)S(1)} %copy-done.60), channel_id=1, source_target_pairs={{0,3},{1,0},{2,1},{3,2},{32,35},{33,32},{34,33},{35,34},{64,67},{6... | collective-permute-start | bytes 3244040 | tf_op jit(solution)/shard_map/ppermute | solution.py:69
  483.0 20.7 %collective-permute-start.66 = (bf16[272,1024]{1,0:T(8,128)(2,1)S(1)}, bf16[272,1024]{1,0:T(8,128)(2,1)S(1)}, u32[]{:S(2)}, u32[]{:S(2)}) collective-permute-start(bf16[272,1024]{1,0:T(8,128)(2,1)S(1)} %pad_maximum_fusion.1), channel_id=1, source_target_pairs={{0,1},{1,2},{2,3},{3,0},{32,33},{33,34},{34,35},{35,32},{64,65},{6... | collective-permute-start | bytes 1671176 | tf_op jit(solution)/shard_map/ppermute | solution.py:69
  492.8 22.4 %collective-permute-start.79 = (bf16[128,1024]{1,0:T(8,128)(2,1)S(1)}, bf16[128,1024]{1,0:T(8,128)(2,1)}, u32[]{:S(2)}, u32[]{:S(2)}) collective-permute-start(bf16[128,1024]{1,0:T(8,128)(2,1)S(1)} %pad_maximum_fusion.9), channel_id=1, source_target_pairs={{0,3},{1,0},{2,1},{3,2},{32,35},{33,32},{34,33},{35,34},{64,67},{6... | collective-permute-start | bytes 786440 | tf_op jit(solution)/shard_map/ppermute | solution.py:69
  (119 other events, 508.7 us)
where the time goes:
time: 554 us; the launch traced here: 544 us
  waiting for transfers between devices  303 us (55%)
  starting transfers between devices  107 us (19%)
  Pallas kernels  79.6 us (14%)
  local copies, waits for them, and re-layouts  43.6 us (8%)
  other arithmetic  7.53 us (1%)
    ppermute x44, waiting for transfers between devices, hop(): return lax.ppermute(value, EVERY, pairs)  188 us
    ppermute x34, waiting for transfers between devices, turn(): return lax.ppermute(value, GROUP, pairs)  110 us
    ppermute x34, starting transfers between devices, turn(): return lax.ppermute(value, GROUP, pairs)  60.9 us
    pallas_call x1, Pallas kernels, forward(): pl.pallas_call(partial(forward_kernel, layout, dims), grid=(MICRO,), in_s...  40.8 us
    ppermute x44, starting transfers between devices, hop(): return lax.ppermute(value, EVERY, pairs)  35.3 us
    unnamed x131, local copies, waits for them, and re-layouts  29.6 us
    pallas_call x16, Pallas kernels, backward(): pl.pallas_call(partial(backward_kernel, micro), in_specs=[pl.BlockSpec(me...  24.9 us
    pallas_call x1, Pallas kernels, collect(): pl.pallas_call(partial(collect_kernel, sections, dims, counts), in_specs=...  13.9 us
  transfers between devices with their start and end apart: 82, of which 24 were waited for; matrix products, arithmetic and copies ran while one was open for 3% of the time, Pallas kernels for 3%

commit v1 on v0

--- a/solution.py
+++ b/solution.py
@@ -89,38 +89,84 @@
 
 def ring(value, axis, head):
     size, half = group_dims()[axis], (value.shape[0] - head) // 2
-    pieces = [(0, 0, value, head)]
-    heads = [value[:head]]
+    both = (head, head + half)
+    pieces, heads = [(0, value, both)], [value[:head]]
     if size == 2:
         other = turn(value, axis, 1)
-        pieces.append((1, 0, other, head))
+        pieces.append((1, other, both))
         heads.append(other[:head])
     if size == 4:
         behind, ahead = turn(value, axis, 1), turn(value, axis, -1)
         up = turn(behind[: head + half], axis, 1)
         down = turn(ahead[head + half :], axis, -1)
-        pieces += [(1, 0, ahead, head), (2, 0, up, head), (2, half, down, 0), (3, 0, behind, head)]
+        pieces += [(1, ahead, both), (2, up, (head, None)), (2, down, (None, 0)), (3, behind, both)]
         heads += [ahead[:head], behind[:head], up[:head]]
     return pieces, sum(heads[1:], heads[0])
 
 
-def gather_weights(shard, gain):
-    share = shard.shape[1]
-    value = jnp.concatenate([gain, shard.reshape(4 * share, WIDTH)])
-    pair, gain = ring(value, 0, HEAD_ROWS)
-    firsts = []
-    for begin, axis in ((0, 1), (2 * share, 2)):
-        parts = [piece[at + begin : at + begin + 2 * share] for _, _, piece, at in pair]
-        head = HEAD_ROWS if begin == 0 else 0
-        found, heads = ring(jnp.concatenate(([gain] if head else []) + parts), axis, head)
-        gain = heads if head else gain
-        rows = [piece[at:] for _, _, piece, at in found]
-        firsts.append((rows, head))
-    values = [jnp.concatenate(([gain] if head else []) + rows) for rows, head in firsts]
-    values = [tie(values[0], values[1]), tie(values[1], values[0])]
-    first, gain = ring(values[0], 2, HEAD_ROWS)
-    second, _ = ring(values[1], 1, 0)
-    return [first, second], gain
+def arrange_kernel(layouts, dims, *refs):
+    spot, refs = refs[0], refs[1:]
+    count = sum(len(layout) + (axis == 2) for axis, layout in layouts)
+    ins, outs, sems = refs[:count], refs[count : count + 2], refs[count + 2]
+    copies, offset = [], 0
+    for out, (axis, layout) in zip(outs, layouts):
+        head, size = int(axis == 2), dims[axis]
+        if head:
+            copies.append((ins[offset], out.at[pl.ds(0, 1)]))
+            offset += 1
+        for place, begins in layout:
+            for m, begin in enumerate(begins):
+                for plane in range(dims[0]):
+                    if begin is not None:
+                        to = head + (m * dims[0] + plane) * size
+                        to += lax.rem(spot[axis] + place, size)
+                        source = ins[offset].at[pl.ds(begin + plane, 1)]
+                        copies.append((source, out.at[pl.ds(to, 1)]))
+            offset += 1
+    copies = [
+        pltpu.make_async_copy(source, target, sems.at[at])
+        for at, (source, target) in enumerate(copies)
+    ]
+    for copy in copies:
+        copy.start()
+    for copy in copies:
+        copy.wait()
+
+
+def arrange(spot, rings):
+    dims = group_dims()
+    operands, layouts, shapes = [], [], []
+    for axis, head, pieces in rings:
+        operands += ([] if head is None else [head]) + [piece for _, piece, _ in pieces]
+        layouts.append((axis, [(place, begins) for place, _, begins in pieces]))
+        units = (head is not None) + 2 * dims[0] * dims[axis]
+        shapes.append(pltpu.HBM((units,) + pieces[0][1].shape[1:], jnp.bfloat16))
+    return pl.pallas_call(
+        partial(arrange_kernel, layouts, dims),
+        in_specs=[pl.BlockSpec(memory_space=pltpu.SMEM)]
+        + [pl.BlockSpec(memory_space=pl.ANY)] * len(operands),
+        out_specs=[pl.BlockSpec(memory_space=pl.ANY)] * 2,
+        out_shape=shapes,
+        scratch_shapes=[pltpu.SemaphoreType.DMA((sum(shape.shape[0] for shape in shapes),))],
+        name="arrange",
+    )(spot, *operands)
+
+
+def gather_weights(shard, gain, spot):
+    value = jnp.concatenate([gain, shard])
+    gains, planes = gain, [value]
+    if group_dims()[0] == 2:
+        other = turn(value, 0, 1)
+        gains = gain + other[:1]
+        planes = [jnp.where(spot[0] == 0, value, other), jnp.where(spot[0] == 0, other, value)]
+    rows = [plane[1 + m : 2 + m] for m in range(4) for plane in planes]
+    half = len(rows) // 2
+    first, gains = ring(jnp.concatenate([gains] + rows[:half]), 2, 1)
+    second, _ = ring(jnp.concatenate(rows[half:]), 1, 0)
+    first, second = arrange(spot, [(2, gains, first), (1, None, second)])
+    first, gains = ring(first, 1, 1)
+    second, _ = ring(second, 2, 0)
+    return [first, second], gains
 
 
 def normed(x, gain):
@@ -137,26 +183,25 @@
     w, h5, q3, k5, v5, barred, sems = refs[17:]
     step = pl.program_id(0)
     planes, size_y, size_x = dims
-    z, y, x = spot[0], spot[1], spot[2]
 
     def loads(pair):
         copies, offset = [], sum(len(pieces) for pieces in layout[:pair])
-        share = WIDTH // (planes * size_y * size_x)
-        for at, (place, first, begin, rows) in enumerate(layout[pair]):
-            for row in range(rows // (2 * share)):
-                one, plane = divmod(first // (2 * share) + row, planes)
-                ahead_y, ahead_x = (one, place) if pair == 0 else (place, one)
-                to = lax.rem(z + plane, planes) * size_y + lax.rem(y + ahead_y, size_y)
-                to = to * size_x + lax.rem(x + ahead_x, size_x)
-                to = pl.ds(pl.multiple_of(to * share, share), share)
-                for m in range(2):
-                    source = pieces[offset + at].at[pl.ds(begin + (2 * row + m) * share, share), :]
-                    copies.append(
-                        pltpu.make_async_copy(
-                            source, w.at[2 * pair + m, to, :], sems.at[pair, len(copies)]
+        axis, units = (1, size_x) if pair == 0 else (2, size_y)
+        for at, (place, begins) in enumerate(layout[pair]):
+            to = lax.rem(spot[axis] + place, dims[axis])
+            for m, begin in enumerate(begins):
+                for plane in range(planes):
+                    if begin is not None:
+                        target = w.at[2 * pair + m, plane]
+                        target = target.at[to] if pair == 0 else target.at[:, to]
+                        source = pieces[offset + at].at[pl.ds(begin + plane * units, units)]
+                        copies.append(
+                            pltpu.make_async_copy(source, target, sems.at[pair, len(copies)])
                         )
-                    )
         return copies
+
+    def projection(m, cols):
+        return w[m, :, :, :, :, cols].reshape(WIDTH, 256)
 
     def store(pair):
         half = pl.ds(2 * pair, 2)
@@ -180,8 +225,8 @@
 
     for n in range(0, WIDTH, 256):
         cols = slice(n, n + 256)
-        q3[:, cols] = dot(h5[2 * BLOCK :, :], w[0, :, cols]).astype(jnp.bfloat16)
-        k5[:, cols] = dot(h5[...], w[1, :, cols]).astype(jnp.bfloat16)
+        q3[:, cols] = dot(h5[2 * BLOCK :, :], projection(0, cols)).astype(jnp.bfloat16)
+        k5[:, cols] = dot(h5[...], projection(1, cols)).astype(jnp.bfloat16)
 
     @pl.when(step == 0)
     def _():
@@ -191,7 +236,7 @@
 
     for n in range(0, WIDTH, 256):
         cols = slice(n, n + 256)
-        v5[:, cols] = dot(h5[...], w[2, :, cols]).astype(jnp.bfloat16)
+        v5[:, cols] = dot(h5[...], projection(2, cols)).astype(jnp.bfloat16)
     q_out[0] = q3[...]
     k_out[0] = k5[: 3 * BLOCK, :]
     v_out[0] = v5[: 3 * BLOCK, :]
@@ -218,7 +263,8 @@
             if j == 0:
                 p_out[0, head] = p
                 a_out[0, :, cols] = mixed.astype(jnp.bfloat16)
-            pt_out[0, head, :, rows] = p[:, (2 - j) * BLOCK : (3 - j) * BLOCK].T
+            own_keys = slice((2 - j) * BLOCK, (3 - j) * BLOCK)
+            pt_out[0, head, :, rows] = p[:, own_keys].T
 
     @pl.when(step == MICRO - 1)
     def _():
@@ -228,13 +274,10 @@
 
 def forward(spot, pairs, parts, gain, seg_col, seg_row):
     anywhere = pl.BlockSpec(memory_space=pl.ANY)
-    pieces = [piece for pair in pairs for _, _, piece, _ in pair]
-    layout = [
-        [(place, first, begin, piece.shape[0] - begin) for place, first, piece, begin in pair]
-        for pair in pairs
-    ]
+    pieces = [piece for pair in pairs for _, piece, _ in pair]
+    layout = [[(place, begins) for place, _, begins in pair] for pair in pairs]
     dims = group_dims()
-    most = 2 * dims[0] * dims[1] * dims[2]
+    wide = (4, *dims, WIDTH // (dims[0] * dims[1] * dims[2]), WIDTH)
 
     def per_micro(shape):
         return pl.BlockSpec((1,) + shape, lambda m: (m,) + (0,) * len(shape))
@@ -264,16 +307,16 @@
             per_micro((1, 5 * BLOCK)),
         ],
         out_specs=[anywhere] + [per_micro(shape) for shape, _ in outs],
-        out_shape=[jax.ShapeDtypeStruct((4, WIDTH, WIDTH), jnp.bfloat16)]
+        out_shape=[jax.ShapeDtypeStruct(wide, jnp.bfloat16)]
         + [jax.ShapeDtypeStruct((MICRO,) + shape, kind) for shape, kind in outs],
         scratch_shapes=[
-            pltpu.VMEM((4, WIDTH, WIDTH), jnp.bfloat16),
+            pltpu.VMEM(wide, jnp.bfloat16),
             pltpu.VMEM((5 * BLOCK, WIDTH), jnp.bfloat16),
             pltpu.VMEM((3 * BLOCK, WIDTH), jnp.bfloat16),
             pltpu.VMEM((5 * BLOCK, WIDTH), jnp.bfloat16),
             pltpu.VMEM((5 * BLOCK, WIDTH), jnp.bfloat16),
             pltpu.VMEM((3 * BLOCK, 3 * BLOCK), jnp.float32),
-            pltpu.SemaphoreType.DMA((3, most)),
+            pltpu.SemaphoreType.DMA((3, 16)),
         ],
         compiler_params=pltpu.CompilerParams(vmem_limit_bytes=44 * MIB),
         cost_estimate=pl.CostEstimate(
@@ -626,10 +669,10 @@
     dp = lax.axis_index("dp")
     spot = jnp.stack([dp // size_y, dp % size_y, lax.axis_index("fsdp")]).astype(jnp.int32)
     spread = lax.dynamic_update_slice(
-        jnp.zeros((HEAD_ROWS, WIDTH), jnp.bfloat16), gains, (0, block * share)
+        jnp.zeros((1, share, WIDTH), jnp.bfloat16), gains[None], (0, 0, block * share)
     )
-    pairs, gain = gather_weights(weights[0], spread)
-    gain = jnp.broadcast_to(gain[0:1].astype(jnp.float32), (8, WIDTH))
+    pairs, gain = gather_weights(weights[0], spread, spot)
+    gain = jnp.broadcast_to(gain[0, 0:1].astype(jnp.float32), (8, WIDTH))
 
     x = checkpoints[0]
     left, right = shift(x, 1), shift(x, -1)
@@ -641,24 +684,22 @@
     gathered, h, q, k, v, p, pt, o, a = forward(
         spot, pairs, parts, gain, segs[:, :, None], segs[:, None, :]
     )
+    gathered = gathered.reshape(4, WIDTH, WIDTH)
     kept = (q, k, v, p, pt, o)
 
     kept_grads = [[None] * MICRO for _ in range(sections)]
-    incoming = [[part[micro] for part in cot] for micro in range(MICRO)]
+    arriving, behind = ([part[micro] for part in cot] for micro in range(MICRO))
     for at in range(sections - 1, -1, -1):
         flag = (section == at).astype(jnp.int32).reshape(1)
-        for micro in range(MICRO):
-            grads = list(backward(micro, flag, incoming[micro], gathered, kept, x, gain))
-            if at > 0:
-                before = incoming[micro - 1] if micro > 0 else []
-                if at % 2 == 1:
-                    grads[0] = tie(grads[0], *before)
-                    incoming[micro] = [hop(grads[0], at, at - 1, back) for back in range(3)]
-                else:
-                    grads[0] = tie(grads[0], *before[:1])
-                    own = tie(hop(grads[0], at, at - 1, 0), *before[1:])
-                    incoming[micro] = [own] + [hop(own, at - 1, at - 1, back) for back in (1, 2)]
-            kept_grads[at][micro] = grads
+        first = list(backward(0, flag, arriving, gathered, kept, x, gain))
+        leaving = first[0]
+        if at > 0:
+            arriving = [hop(leaving, at, at - 1, back) for back in (2, 1, 0)][::-1]
+        if at < sections - 1:
+            second[0] = tie(second[0], arriving[0] if at > 0 else leaving)
+            behind = [hop(second[0], at + 1, at, back) for back in (2, 1, 0)][::-1]
+        second = list(backward(1, flag, behind, gathered, kept, x, gain))
+        kept_grads[at] = [first, second]
 
     place = section.astype(jnp.int32).reshape(1)
     frame, gain_part, parts = collect(place, spot, h, a, kept_grads)

time: 554 us -> 549 us (level)
  Pallas kernels: 79.6 us -> 148 us
  waiting for transfers between devices: 303 us -> 261 us
  local copies, waits for them, and re-layouts: 43.6 us -> 22.9 us
  starting transfers between devices: 107 us -> 94.4 us
    pallas_call x0 -> x1, Pallas kernels: none -> 67.6 us  [arrange(): pl.pallas_call(partial(arrange_kernel, layouts, dims), in_specs=[pl.Block...]
    ppermute x44, waiting for transfers between devices: 188 us -> 155 us  [hop(): return lax.ppermute(value, EVERY, pairs)]
    unnamed x131 -> x69, local copies, waits for them, and re-layouts: 29.6 us -> 11.7 us
    ppermute x34, starting transfers between devices: 60.9 us -> 46 us  [turn(): return lax.ppermute(value, GROUP, pairs)]
    ppermute x34, waiting for transfers between devices: 110 us -> 99.3 us  [turn(): return lax.ppermute(value, GROUP, pairs)]
    pallas_call x16, Pallas kernels: 24.9 us -> 32 us  [backward(): pl.pallas_call(partial(backward_kernel, micro), in_specs=[pl.BlockSpec(me...]
    pallas_call x1, Pallas kernels: 40.8 us -> 34.8 us  [forward(): pl.pallas_call(partial(forward_kernel, layout, dims), grid=(MICRO,), in_s...]
  transfers between devices with their start and end apart: 82 -> 82, of which waited for: 24 -> 26; matrix products, arithmetic and copies ran while one was open for 3% -> 3% of each run, Pallas kernels for 3% -> 4%
where the time goes in v1:
time: 549 us; the launch traced here: 539 us
  waiting for transfers between devices  261 us (48%)
  Pallas kernels  148 us (27%)
  starting transfers between devices  94.4 us (17%)
  local copies, waits for them, and re-layouts  22.9 us (4%)
  other arithmetic  9.54 us (2%)
    ppermute x44, waiting for transfers between devices, hop(): return lax.ppermute(value, EVERY, pairs)  155 us
    ppermute x34, waiting for transfers between devices, turn(): return lax.ppermute(value, GROUP, pairs)  99.3 us
    pallas_call x1, Pallas kernels, arrange(): pl.pallas_call(partial(arrange_kernel, layouts, dims), in_specs=[pl.Block...  67.6 us
    ppermute x34, starting transfers between devices, turn(): return lax.ppermute(value, GROUP, pairs)  46 us
    ppermute x44, starting transfers between devices, hop(): return lax.ppermute(value, EVERY, pairs)  35 us
    pallas_call x1, Pallas kernels, forward(): pl.pallas_call(partial(forward_kernel, layout, dims), grid=(MICRO,), in_s...  34.8 us
    pallas_call x16, Pallas kernels, backward(): pl.pallas_call(partial(backward_kernel, micro), in_specs=[pl.BlockSpec(me...  32 us
    pallas_call x1, Pallas kernels, collect(): pl.pallas_call(partial(collect_kernel, sections, dims, counts), in_specs=...  13.9 us
  transfers between devices with their start and end apart: 82, of which 26 were waited for; matrix products, arithmetic and copies ran while one was open for 3% of the time, Pallas kernels for 4%

profile of v1, /device:TPU:6, one launch (start us, length us, event | category | flops | bytes accessed | tf_op | source)
XLA Modules:
  0.0 539.0 jit_solution(15640725470112910728)
XLA Ops:
  4.6 7.7 %collective-permute-done = bf16[5,32,1024]{2,1,0:T(8,128)(2,1)S(1)} collective-permute-done((bf16[5,32,1024]{2,1,0:T(8,128)(2,1)S(1)}, bf16[5,32,1024]{2,1,0:T(8,128)(2,1)S(1)}, u32[]{:S(2)}, u32[]{:S(2)}) %collective-permute-start) | collective-permute-done | bytes 327712 | tf_op jit(solution)/shard_map/ppermute | solution.py:69
  18.9 3.4 collective-permute-done.2.refs_6_
  34.9 67.6 %arrange.1 = (bf16[17,32,1024]{2,1,0:T(8,128)(2,1)}, bf16[16,32,1024]{2,1,0:T(8,128)(2,1)}) custom-call(s32[3]{0:T(128)} %pad_add_fusion.refs_0_.refs_1_, bf16[1,32,1024]{2,1,0:T(8,128)(2,1)} %slice_add_fusion.refs_1_, bf16[5,32,1024]{2,1,0:T(8,128)(2,1)} %copy-done.26, bf16[5,32,1024]{2,1,0:T(8,128)(2,1)} %copy-done.22, bf16[3,32,1024]{2,1,0:T(8,128)(2,1)} %copy-done.27, ...), custom_call_target="tpu_custom_call" | custom-call | tf_op jit(solution)/shard_map/arrange/pallas_call | solution.py:144
  112.3 14.9 %collective-permute-done.10.refs_5_ = bf16[17,32,1024]{2,1,0:T(8,128)(2,1)} collective-permute-done((bf16[17,32,1024]{2,1,0:T(8,128)(2,1)}, bf16[17,32,1024]{2,1,0:T(8,128)(2,1)}, u32[]{:S(2)}, u32[]{:S(2)}) %collective-permute-start.10) | collective-permute-done | bytes 1114144 | tf_op jit(solution)/shard_map/ppermute | solution.py:69
  131.1 5.2 collective-permute-done.17.refs_12_
  143.3 6.6 %collective-permute-start.18 = (bf16[2,128,1024]{2,1,0:T(8,128)(2,1)}, bf16[2,128,1024]{2,1,0:T(8,128)(2,1)S(1)}, u32[]{:S(2)}, u32[]{:S(2)}) collective-permute-start(bf16[2,128,1024]{2,1,0:T(8,128)(2,1)} %collective-permute-done.17.refs_12_), channel_id=1, source_target_pairs={{0,1},{1,2},{2,3},{3,32},{32,33},{33,34},{34,35},{35,64},{64,65},{... | collective-permute-start | bytes 1572872 | tf_op jit(solution)/shard_map/ppermute | solution.py:38
  155.1 5.4 collective-permute-start.12
  168.0 5.7 %collective-permute-done.16.refs_9_ = bf16[8,32,1024]{2,1,0:T(8,128)(2,1)S(1)} collective-permute-done((bf16[8,32,1024]{2,1,0:T(8,128)(2,1)S(1)}, bf16[8,32,1024]{2,1,0:T(8,128)(2,1)S(1)}, u32[]{:S(2)}, u32[]{:S(2)}) %collective-permute-start.16) | collective-permute-done | bytes 524320 | tf_op jit(solution)/shard_map/ppermute | solution.py:69
  176.8 34.8 %forward.1 = (bf16[4,2,4,4,32,1024]{5,4,3,2,1,0:T(8,128)(2,1)}, bf16[2,128,1024]{2,1,0:T(8,128)(2,1)S(1)}, bf16[2,384,1024]{2,1,0:T(8,128)(2,1)}, bf16[2,384,102...) custom-call(s32[3]{0:T(128)S(1)} %copy-done.16, ...), custom_call_target="tpu_custom_call" | custom-call | flops 8053063680 | bytes 29360128 | tf_op jit(solution)/shard_map/forward/pallas_call | solution.py:298
  258.1 111.5 %collective-permute-done.41.refs_1_ = bf16[128,1024]{1,0:T(8,128)(2,1)S(1)} collective-permute-done((bf16[128,1024]{1,0:T(8,128)(2,1)}, bf16[128,1024]{1,0:T(8,128)(2,1)S(1)}, u32[]{:S(2)}, u32[]{:S(2)}) %collective-permute-start.41) | collective-permute-done | bytes 262176 | tf_op jit(solution)/shard_map/ppermute | solution.py:49
  372.3 17.3 %collective-permute-done.42.refs_2_ = bf16[128,1024]{1,0:T(8,128)(2,1)S(1)} collective-permute-done((bf16[128,1024]{1,0:T(8,128)(2,1)}, bf16[128,1024]{1,0:T(8,128)(2,1)S(1)}, u32[]{:S(2)}, u32[]{:S(2)}) %collective-permute-start.42) | collective-permute-done | bytes 262176 | tf_op jit(solution)/shard_map/ppermute | solution.py:49
  389.6 4.0 collective-permute-done.43.refs_3_
  394.5 10.2 %backward.23 = (bf16[128,1024]{1,0:T(8,128)(2,1)}, bf16[128,1024]{1,0:T(8,128)(2,1)}, bf16[128,1024]{1,0:T(8,128)(2,1)}, bf16[128,1024]{1,0:T(8,128)(2,1)}, bf16...) custom-call(s32[1]{0:T(128)} %bitcast.9.refs_0_, bf16[128,1024]{1,0:T(8,128)(2,1)S(1)} %copy-done.11, ...), custom_call_target="tpu_custom_call" | custom-call | flops 1879048192 | bytes 16777216 | tf_op jit(solution)/shard_map/backward/pallas_call | solution.py:442
  409.0 11.4 %collective-permute-done.62.refs_1_ = bf16[128,1024]{1,0:T(8,128)(2,1)S(1)} collective-permute-done((bf16[128,1024]{1,0:T(8,128)(2,1)}, bf16[128,1024]{1,0:T(8,128)(2,1)S(1)}, u32[]{:S(2)}, u32[]{:S(2)}) %collective-permute-start.62) | collective-permute-done | bytes 262176 | tf_op jit(solution)/shard_map/ppermute | solution.py:49
  420.5 7.6 %collective-permute-done.63.refs_2_ = bf16[128,1024]{1,0:T(8,128)(2,1)S(1)} collective-permute-done((bf16[128,1024]{1,0:T(8,128)(2,1)}, bf16[128,1024]{1,0:T(8,128)(2,1)S(1)}, u32[]{:S(2)}, u32[]{:S(2)}) %collective-permute-start.63) | collective-permute-done | bytes 262176 | tf_op jit(solution)/shard_map/ppermute | solution.py:49
  431.1 10.2 %backward.31 = (bf16[128,1024]{1,0:T(8,128)(2,1)}, bf16[128,1024]{1,0:T(8,128)(2,1)}, bf16[128,1024]{1,0:T(8,128)(2,1)}, bf16[128,1024]{1,0:T(8,128)(2,1)}, bf16...) custom-call(s32[1]{0:T(128)} %bitcast.9.refs_0_, bf16[128,1024]{1,0:T(8,128)(2,1)S(1)} %collective-permute-done.62.refs_1_, ...), custom_call_target="tpu_custom_call" | custom-call | flops 1879048192 | bytes 16777216 | tf_op jit(solution)/shard_map/backward/pallas_call | solution.py:442
  441.3 13.9 %collect.1 = (bf16[2,128,1024]{2,1,0:T(8,128)(2,1)}, bf16[16,1024]{1,0:T(8,128)(2,1)S(1)}, bf16[512,1024]{1,0:T(8,128)(2,1)S(1)}, bf16[528,1024]{1,0:T(8,128)(2,...) custom-call(s32[1]{0:T(128)} %bitcast.refs_0_, ...), custom_call_target="tpu_custom_call" | custom-call | flops 2147483648 | bytes 14680064 | tf_op jit(solution)/shard_map/collect/pallas_call | solution.py:597
  458.5 18.6 %collective-permute-done.73 = bf16[512,1024]{1,0:T(8,128)(2,1)S(1)} collective-permute-done((bf16[512,1024]{1,0:T(8,128)(2,1)}, bf16[512,1024]{1,0:T(8,128)(2,1)S(1)}, u32[]{:S(2)}, u32[]{:S(2)}) %collective-permute-start.73) | collective-permute-done | bytes 1048608 | tf_op jit(solution)/shard_map/ppermute | solution.py:69
  490.9 8.0 %collective-permute-done.67 = bf16[528,1024]{1,0:T(8,128)(2,1)S(1)} collective-permute-done((bf16[528,1024]{1,0:T(8,128)(2,1)S(1)}, bf16[528,1024]{1,0:T(8,128)(2,1)S(1)}, u32[]{:S(2)}, u32[]{:S(2)}) %collective-permute-start.67) | collective-permute-done | bytes 1081376 | tf_op jit(solution)/shard_map/ppermute | solution.py:69
  503.5 6.4 %collective-permute-done.68 = bf16[256,1024]{1,0:T(8,128)(2,1)S(1)} collective-permute-done((bf16[256,1024]{1,0:T(8,128)(2,1)S(1)}, bf16[256,1024]{1,0:T(8,128)(2,1)S(1)}, u32[]{:S(2)}, u32[]{:S(2)}) %collective-permute-start.68) | collective-permute-done | bytes 524320 | tf_op jit(solution)/shard_map/ppermute | solution.py:69
  514.9 3.4 collective-permute-done.69
  519.2 5.8 %collective-permute-done.70 = bf16[80,1024]{1,0:T(8,128)(2,1)S(1)} collective-permute-done((bf16[80,1024]{1,0:T(8,128)(2,1)S(1)}, bf16[80,1024]{1,0:T(8,128)(2,1)S(1)}, u32[]{:S(2)}, u32[]{:S(2)}) %collective-permute-start.70) | collective-permute-done | bytes 163872 | tf_op jit(solution)/shard_map/ppermute | solution.py:69
  525.2 4.9 collective-permute-done.72
  530.4 6.7 %collective-permute-done.81 = bf16[144,1024]{1,0:T(8,128)(2,1)S(1)} collective-permute-done((bf16[144,1024]{1,0:T(8,128)(2,1)S(1)}, bf16[144,1024]{1,0:T(8,128)(2,1)S(1)}, u32[]{:S(2)}, u32[]{:S(2)}) %collective-permute-start.81) | collective-permute-done | bytes 294944 | tf_op jit(solution)/shard_map/ppermute | solution.py:69
  (304 shorter events, 145.3 us)
Async XLA Ops:
  102.5 24.7 %collective-permute-start.10 = (bf16[17,32,1024]{2,1,0:T(8,128)(2,1)}, bf16[17,32,1024]{2,1,0:T(8,128)(2,1)}, u32[]{:S(2)}, u32[]{:S(2)}) collective-permute-start(bf16[17,32,1024]{2,1,0:T(8,128)(2,1)} %get-tuple-element.122.refs_1_), channel_id=1, source_target_pairs={{0,32},{1,33},{2,34},{3,35},{32,64},{33,65},{34,66},{35,67},{64,96... | collective-permute-start | bytes 3342344 | tf_op jit(solution)/shard_map/ppermute | solution.py:69
  103.0 34.8 %collective-permute-start.13 = (bf16[16,32,1024]{2,1,0:T(8,128)(2,1)}, bf16[16,32,1024]{2,1,0:T(8,128)(2,1)S(1)}, u32[]{:S(2)}, u32[]{:S(2)}) collective-permute-start(bf16[16,32,1024]{2,1,0:T(8,128)(2,1)} %get-tuple-element.123.refs_6_), channel_id=1, source_target_pairs={{0,3},{1,0},{2,1},{3,2},{32,35},{33,32},{34,33},{35,34},{64,67},{6... | collective-permute-start | bytes 3145736 | tf_op jit(solution)/shard_map/ppermute | solution.py:69
  103.0 36.3 %collective-permute-start.14 = (bf16[16,32,1024]{2,1,0:T(8,128)(2,1)}, bf16[16,32,1024]{2,1,0:T(8,128)(2,1)S(1)}, u32[]{:S(2)}, u32[]{:S(2)}) collective-permute-start(bf16[16,32,1024]{2,1,0:T(8,128)(2,1)} %get-tuple-element.123.refs_6_), channel_id=1, source_target_pairs={{0,1},{1,2},{2,3},{3,0},{32,33},{33,34},{34,35},{35,32},{64,65},{6... | collective-permute-start | bytes 3145736 | tf_op jit(solution)/shard_map/ppermute | solution.py:69
  106.2 30.1 %collective-permute-start.17 = (bf16[2,128,1024]{2,1,0:T(8,128)(2,1)S(1)}, bf16[2,128,1024]{2,1,0:T(8,128)(2,1)}, u32[]{:S(2)}, u32[]{:S(2)}) collective-permute-start(bf16[2,128,1024]{2,1,0:T(8,128)(2,1)S(1)} %bitcast.125), channel_id=1, source_target_pairs={{0,1},{1,2},{2,3},{3,32},{32,33},{33,34},{34,35},{35,64},{64,65},{... | collective-permute-start | bytes 1572872 | tf_op jit(solution)/shard_map/ppermute | solution.py:38
  109.1 40.8 %collective-permute-start.9 = (bf16[17,32,1024]{2,1,0:T(8,128)(2,1)}, bf16[17,32,1024]{2,1,0:T(8,128)(2,1)}, u32[]{:S(2)}, u32[]{:S(2)}) collective-permute-start(bf16[17,32,1024]{2,1,0:T(8,128)(2,1)} %get-tuple-element.122.refs_1_), channel_id=1, source_target_pairs={{0,96},{1,97},{2,98},{3,99},{32,0},{33,1},{34,2},{35,3},{64,32},{6... | collective-permute-start | bytes 3342344 | tf_op jit(solution)/shard_map/ppermute | solution.py:69
  136.3 16.6 %collective-permute-start.21 = (bf16[2,128,1024]{2,1,0:T(8,128)(2,1)S(1)}, bf16[2,128,1024]{2,1,0:T(8,128)(2,1)}, u32[]{:S(2)}, u32[]{:S(2)}) collective-permute-start(bf16[2,128,1024]{2,1,0:T(8,128)(2,1)S(1)} %copy-done.25), channel_id=1, source_target_pairs={{21,28},{22,29},{23,30},{52,31},{53,60},{54,61},{55,62},{84,63},{8... | collective-permute-start | bytes 1572872 | tf_op jit(solution)/shard_map/ppermute | solution.py:49
  143.3 22.7 %collective-permute-start.18 = (bf16[2,128,1024]{2,1,0:T(8,128)(2,1)}, bf16[2,128,1024]{2,1,0:T(8,128)(2,1)S(1)}, u32[]{:S(2)}, u32[]{:S(2)}) collective-permute-start(bf16[2,128,1024]{2,1,0:T(8,128)(2,1)} %collective-permute-done.17.refs_12_), channel_id=1, source_target_pairs={{0,1},{1,2},{2,3},{3,32},{32,33},{33,34},{34,35},{35,64},{64,65},{... | collective-permute-start | bytes 1572872 | tf_op jit(solution)/shard_map/ppermute | solution.py:38
  149.9 18.1 %collective-permute-start.20 = (bf16[2,128,1024]{2,1,0:T(8,128)(2,1)}, bf16[2,128,1024]{2,1,0:T(8,128)(2,1)S(1)}, u32[]{:S(2)}, u32[]{:S(2)}) collective-permute-start(bf16[2,128,1024]{2,1,0:T(8,128)(2,1)} %collective-permute-done.19.refs_14_), channel_id=1, source_target_pairs={{1,0},{2,1},{3,2},{32,3},{33,32},{34,33},{35,34},{64,35},{65,64},{... | collective-permute-start | bytes 1572872 | tf_op jit(solution)/shard_map/ppermute | solution.py:38
  153.1 20.6 %collective-permute-start.16 = (bf16[8,32,1024]{2,1,0:T(8,128)(2,1)S(1)}, bf16[8,32,1024]{2,1,0:T(8,128)(2,1)S(1)}, u32[]{:S(2)}, u32[]{:S(2)}) collective-permute-start(bf16[8,32,1024]{2,1,0:T(8,128)(2,1)S(1)} %slice.348), channel_id=1, source_target_pairs={{0,3},{1,0},{2,1},{3,2},{32,35},{33,32},{34,33},{35,34},{64,67},{6... | collective-permute-start | bytes 1572872 | tf_op jit(solution)/shard_map/ppermute | solution.py:69
  155.1 21.7 %collective-permute-start.12 = (bf16[8,32,1024]{2,1,0:T(8,128)(2,1)S(1)}, bf16[8,32,1024]{2,1,0:T(8,128)(2,1)S(1)}, u32[]{:S(2)}, u32[]{:S(2)}) collective-permute-start(bf16[8,32,1024]{2,1,0:T(8,128)(2,1)S(1)} %slice.346), channel_id=1, source_target_pairs={{0,96},{1,97},{2,98},{3,99},{32,0},{33,1},{34,2},{35,3},{64,32},{6... | collective-permute-start | bytes 1572872 | tf_op jit(solution)/shard_map/ppermute | solution.py:69
  253.5 116.1 %collective-permute-start.41 = (bf16[128,1024]{1,0:T(8,128)(2,1)}, bf16[128,1024]{1,0:T(8,128)(2,1)S(1)}, u32[]{:S(2)}, u32[]{:S(2)}) collective-permute-start(bf16[128,1024]{1,0:T(8,128)(2,1)} %get-tuple-element.139.refs_16_), channel_id=1, source_target_pairs={{4,0},{5,1},{6,2},{7,3},{36,32},{37,33},{38,34},{39,35},{68,64},{6... | collective-permute-start | bytes 786440 | tf_op jit(solution)/shard_map/ppermute | solution.py:49
  254.8 134.8 %collective-permute-start.42 = (bf16[128,1024]{1,0:T(8,128)(2,1)}, bf16[128,1024]{1,0:T(8,128)(2,1)S(1)}, u32[]{:S(2)}, u32[]{:S(2)}) collective-permute-start(bf16[128,1024]{1,0:T(8,128)(2,1)} %get-tuple-element.139.refs_16_), channel_id=1, source_target_pairs={{5,0},{6,1},{7,2},{36,3},{37,32},{38,33},{39,34},{68,35},{69,64},{... | collective-permute-start | bytes 786440 | tf_op jit(solution)/shard_map/ppermute | solution.py:49
  256.1 137.4 %collective-permute-start.43 = (bf16[128,1024]{1,0:T(8,128)(2,1)}, bf16[128,1024]{1,0:T(8,128)(2,1)S(1)}, u32[]{:S(2)}, u32[]{:S(2)}) collective-permute-start(bf16[128,1024]{1,0:T(8,128)(2,1)} %get-tuple-element.139.refs_16_), channel_id=1, source_target_pairs={{6,0},{7,1},{36,2},{37,3},{38,32},{39,33},{68,34},{69,35},{70,64},... | collective-permute-start | bytes 786440 | tf_op jit(solution)/shard_map/ppermute | solution.py:49
  370.3 34.4 %collective-permute-start.59 = (bf16[128,1024]{1,0:T(8,128)(2,1)}, bf16[128,1024]{1,0:T(8,128)(2,1)S(1)}, u32[]{:S(2)}, u32[]{:S(2)}) collective-permute-start(bf16[128,1024]{1,0:T(8,128)(2,1)} %tie.12.refs_34_), channel_id=1, source_target_pairs={{8,4},{9,5},{10,6},{11,7},{40,36},{41,37},{42,38},{43,39},{72,68},... | collective-permute-start | bytes 786440 | tf_op jit(solution)/shard_map/ppermute | solution.py:49
  371.0 33.8 %collective-permute-start.60 = (bf16[128,1024]{1,0:T(8,128)(2,1)}, bf16[128,1024]{1,0:T(8,128)(2,1)S(1)}, u32[]{:S(2)}, u32[]{:S(2)}) collective-permute-start(bf16[128,1024]{1,0:T(8,128)(2,1)} %tie.12.refs_34_), channel_id=1, source_target_pairs={{9,4},{10,5},{11,6},{40,7},{41,36},{42,37},{43,38},{72,39},{73,68}... | collective-permute-start | bytes 786440 | tf_op jit(solution)/shard_map/ppermute | solution.py:49
  371.7 33.1 %collective-permute-start.61 = (bf16[128,1024]{1,0:T(8,128)(2,1)}, bf16[128,1024]{1,0:T(8,128)(2,1)S(1)}, u32[]{:S(2)}, u32[]{:S(2)}) collective-permute-start(bf16[128,1024]{1,0:T(8,128)(2,1)} %tie.12.refs_34_), channel_id=1, source_target_pairs={{10,4},{11,5},{40,6},{41,7},{42,36},{43,37},{72,38},{73,39},{74,68... | collective-permute-start | bytes 786440 | tf_op jit(solution)/shard_map/ppermute | solution.py:49
  406.4 21.7 %collective-permute-start.63 = (bf16[128,1024]{1,0:T(8,128)(2,1)}, bf16[128,1024]{1,0:T(8,128)(2,1)S(1)}, u32[]{:S(2)}, u32[]{:S(2)}) collective-permute-start(bf16[128,1024]{1,0:T(8,128)(2,1)} %tie.13.refs_22_), channel_id=1, source_target_pairs={{5,0},{6,1},{7,2},{36,3},{37,32},{38,33},{39,34},{68,35},{69,64},{... | collective-permute-start | bytes 786440 | tf_op jit(solution)/shard_map/ppermute | solution.py:49
  407.7 23.4 %collective-permute-start.64 = (bf16[128,1024]{1,0:T(8,128)(2,1)}, bf16[128,1024]{1,0:T(8,128)(2,1)S(1)}, u32[]{:S(2)}, u32[]{:S(2)}) collective-permute-start(bf16[128,1024]{1,0:T(8,128)(2,1)} %tie.13.refs_22_), channel_id=1, source_target_pairs={{6,0},{7,1},{36,2},{37,3},{38,32},{39,33},{68,34},{69,35},{70,64},... | collective-permute-start | bytes 786440 | tf_op jit(solution)/shard_map/ppermute | solution.py:49
  455.1 21.9 %collective-permute-start.73 = (bf16[512,1024]{1,0:T(8,128)(2,1)}, bf16[512,1024]{1,0:T(8,128)(2,1)S(1)}, u32[]{:S(2)}, u32[]{:S(2)}) collective-permute-start(bf16[512,1024]{1,0:T(8,128)(2,1)} %get-tuple-element.238), channel_id=1, source_target_pairs={{0,32},{1,33},{2,34},{3,35},{32,64},{33,65},{34,66},{35,67},{64,96... | collective-permute-start | bytes 3145736 | tf_op jit(solution)/shard_map/ppermute | solution.py:69
  455.2 22.1 %collective-permute-start.75 = (bf16[512,1024]{1,0:T(8,128)(2,1)}, bf16[512,1024]{1,0:T(8,128)(2,1)S(1)}, u32[]{:S(2)}, u32[]{:S(2)}) collective-permute-start(bf16[512,1024]{1,0:T(8,128)(2,1)} %get-tuple-element.239), channel_id=1, source_target_pairs={{0,96},{1,97},{2,98},{3,99},{32,0},{33,1},{34,2},{35,3},{64,32},{6... | collective-permute-start | bytes 3145736 | tf_op jit(solution)/shard_map/ppermute | solution.py:69
  458.5 24.1 %collective-permute-start.65 = (bf16[528,1024]{1,0:T(8,128)(2,1)}, bf16[528,1024]{1,0:T(8,128)(2,1)S(1)}, u32[]{:S(2)}, u32[]{:S(2)}) collective-permute-start(bf16[528,1024]{1,0:T(8,128)(2,1)} %get-tuple-element.231), channel_id=1, source_target_pairs={{0,1},{1,2},{2,3},{3,0},{32,33},{33,34},{34,35},{35,32},{64,65},{6... | collective-permute-start | bytes 3244040 | tf_op jit(solution)/shard_map/ppermute | solution.py:69
  480.9 18.1 %collective-permute-start.67 = (bf16[528,1024]{1,0:T(8,128)(2,1)S(1)}, bf16[528,1024]{1,0:T(8,128)(2,1)S(1)}, u32[]{:S(2)}, u32[]{:S(2)}) collective-permute-start(bf16[528,1024]{1,0:T(8,128)(2,1)S(1)} %copy-done.32), channel_id=1, source_target_pairs={{0,3},{1,0},{2,1},{3,2},{32,35},{33,32},{34,33},{35,34},{64,67},{6... | collective-permute-start | bytes 3244040 | tf_op jit(solution)/shard_map/ppermute | solution.py:69
  482.8 16.1 %collective-permute-start.66 = (bf16[272,1024]{1,0:T(8,128)(2,1)S(1)}, bf16[272,1024]{1,0:T(8,128)(2,1)S(1)}, u32[]{:S(2)}, u32[]{:S(2)}) collective-permute-start(bf16[272,1024]{1,0:T(8,128)(2,1)S(1)} %pad_maximum_fusion.1), channel_id=1, source_target_pairs={{0,1},{1,2},{2,3},{3,0},{32,33},{33,34},{34,35},{35,32},{64,65},{6... | collective-permute-start | bytes 1671176 | tf_op jit(solution)/shard_map/ppermute | solution.py:69
  488.6 22.5 %collective-permute-start.79 = (bf16[128,1024]{1,0:T(8,128)(2,1)S(1)}, bf16[128,1024]{1,0:T(8,128)(2,1)}, u32[]{:S(2)}, u32[]{:S(2)}) collective-permute-start(bf16[128,1024]{1,0:T(8,128)(2,1)S(1)} %pad_maximum_fusion.8), channel_id=1, source_target_pairs={{0,3},{1,0},{2,1},{3,2},{32,35},{33,32},{34,33},{35,34},{64,67},{6... | collective-permute-start | bytes 786440 | tf_op jit(solution)/shard_map/ppermute | solution.py:69
  (91 other events, 813.9 us)
